TPU v7x, 32 devices: a whole 2x2x4 slice. The times are simulated.
32 devices in a mesh: groups: 2 (over y), slab: 4 (over z), side: 4 (over x, core).
Axes of the slice: x: 2, y: 2, z: 4, core: 2. Of those that a mesh axis runs over, the one named last changes fastest.
Arguments:
- populations: float32 [19, 32, 256, 128], P(None, ('groups', 'slab'), 'side'), parts along dimension 1, may hold values from 0.5 to 1.5
- solid_mask: int32 [32, 256, 128], P(('groups', 'slab'), 'side'), parts along dimension 0, may hold values 0 or 1
- point_cell: int32 [65536], P(('groups', 'slab', 'side')), parts along dimension 0, may hold values from 0 to 32767
- point_owner: int32 [65536, 1], P(('groups', 'slab', 'side')), parts along dimension 0, may hold values from 0 to 15; in each aligned block of 2048 rows (0 to 2047, 2048 to 4095, ...) at most 256 rows name the same one
- point_block: int32 [65536], P(('groups', 'slab', 'side')), parts along dimension 0, may hold values from 0 to 7
- point_coords: float32 [3, 65536], P(None, ('groups', 'slab', 'side')), parts along dimension 1, may hold values from 0 to 1
- point_normal: float32 [3, 65536], P(None, ('groups', 'slab', 'side')), parts along dimension 1, may hold values from -1 to 1
- node_coords: float32 [3, 32768], P(None, ('groups', 'slab', 'side')), parts along dimension 1, may hold values from 0 to 1
- struct_prev: float32 [3, 32768], P(None, ('groups', 'slab', 'side')), parts along dimension 1, may hold values from -6 to 6
- compliance: float32 [32768], P(('groups', 'slab', 'side')), parts along dimension 0, may hold values from 0.5 to 2
- elem_nodes: int32 [4, 32768], P(None, ('groups', 'slab', 'side')), parts along dimension 1, may hold values from 0 to 1023
- elem_stiff: float32 [12, 12, 32768], P(None, None, ('groups', 'slab', 'side')), parts along dimension 2, may hold values from -1.75 to 1.75
- iterate: float32 [3, 65536], P(None, ('groups', 'slab', 'side')), parts along dimension 1
- resid_prev: float32 [3, 65536], P(None, ('groups', 'slab', 'side')), parts along dimension 1, may hold values from -6 to 6
- image_prev: float32 [3, 65536], P(None, ('groups', 'slab', 'side')), parts along dimension 1, may hold values from -6 to 6
- resid_history: float32 [4, 3, 65536], P(None, None, ('groups', 'slab', 'side')), parts along dimension 2
- image_history: float32 [4, 3, 65536], P(None, None, ('groups', 'slab', 'side')), parts along dimension 2, may hold values from -6 to 6
Outputs:
- populations_next: float32 [19, 32, 256, 128], P(None, ('groups', 'slab'), 'side'), parts along dimension 1
- struct_disp: float32 [3, 32768], P(None, ('groups', 'slab', 'side')), parts along dimension 1
- iterate_next: float32 [3, 65536], P(None, ('groups', 'slab', 'side')), parts along dimension 1
There are 2 independent parts, one for each index of `groups`. A program takes and returns all parts, laid end to end along the dimension named above; each array names one. Nothing has to cross between parts.
Inputs may be any that keep to these rules, and one draw needn't show every extreme that they name: `point_cell`: cells are numbered within the point's own device's block of 4 x 64 x 128 cells, y fastest. `point_owner`: devices numbered slab * 4 + side; among one device's 2048 points at most 256 name the same owner, and in every draw some owner is named by exactly 256 of them. `point_block`: block number within the owner's 8 blocks. `elem_nodes`: node numbers within the device that holds the element.
All inputs are finite; a program needn't handle non-finite values. No bound on the sum of `solid_mask` on one device may be relied on, other than what follows from the above.
Results may differ from a plain program's by a relative error of at most 0.0003.
Values sent between devices are 32-bit elements; how exact they have to be, the bound alone decides.
A program may use at most 64 MiB of HBM per device.

v0:
```python
import functools

import jax
import jax.numpy as jnp
import numpy as np
from jax import lax
from jax.experimental import pallas as pl
from jax.experimental.pallas import tpu as pltpu
from jax.sharding import PartitionSpec as P

MESH = pl.DeviceIdType.MESH
BLOCK = 128
SUB = 8
PAD = 8
HALO_SLOTS = 8

velocities = np.array(
    [
        [0, 0, 0],
        [1, 0, 0],
        [-1, 0, 0],
        [0, 1, 0],
        [0, -1, 0],
        [0, 0, 1],
        [0, 0, -1],
        [1, 1, 0],
        [-1, -1, 0],
        [1, -1, 0],
        [-1, 1, 0],
        [1, 0, 1],
        [-1, 0, -1],
        [1, 0, -1],
        [-1, 0, 1],
        [0, 1, 1],
        [0, -1, -1],
        [0, 1, -1],
        [0, -1, 1],
    ]
)
lattice_weights = [1.0 / 3.0] + [1.0 / 18.0] * 6 + [1.0 / 36.0] * 12
relax_rate = 1.25
base_density = 19.0
support_scale = 0.1
f32, bf16 = jnp.float32, jnp.bfloat16

z_dirs = {s: [d for d in range(19) if velocities[d, 2] == s] for s in (1, -1)}
x_dirs = {s: [d for d in range(19) if velocities[d, 0] == s] for s in (1, -1)}
corners = [
    (d, int(velocities[d, 0]), int(velocities[d, 2]))
    for d in range(19)
    if velocities[d, 0] != 0 and velocities[d, 2] != 0
]


def pieces(x, count):
    out = []
    for _ in range(count - 1):
        part = x.astype(bf16)
        out.append(part)
        x = x - part.astype(f32)
    out.append(x.astype(bf16))
    return out


def stacked_pieces(x, count):
    out = []
    for _ in range(count - 1):
        part = x.astype(bf16).astype(f32)
        out.append(part)
        x = x - part
    out.append(x)
    return jnp.concatenate(out, axis=0).astype(bf16)


def mm(a, b):
    return jnp.dot(a, b, preferred_element_type=f32)


def mm_nt(a, b):
    return lax.dot_general(a, b, (((1,), (1,)), ((), ())), preferred_element_type=f32)


def rows_iota(rows, columns):
    return lax.broadcasted_iota(jnp.int32, (rows, columns), 0)


def onehot(index, rows):
    return jnp.where(rows_iota(rows, index.shape[1]) == index, 1.0, 0.0).astype(f32)


def fold_lanes(x):
    total = x[:, 0:128]
    for j in range(1, x.shape[1] // 128):
        total = total + x[:, j * 128 : (j + 1) * 128]
    return jnp.sum(total, axis=0, keepdims=True)


def kernel(
    n_slab,
    n_side,
    pop,
    mask,
    cell,
    owner,
    block,
    coords,
    normal,
    nodes,
    sprev,
    comp,
    enodes,
    stiff,
    iterate,
    rprev,
    iprev,
    rhist,
    ihist,
    out_pop,
    out_disp,
    out_iter,
    padded,
    fields,
    zsend,
    zrecv,
    xsend,
    xrecv,
    csend,
    crecv,
    nbuf,
    lsend,
    lrecv,
    dbuf,
    gbuf,
    wide,
    spb,
    dofs,
    force,
    stiffed,
    whi,
    wlo,
    tract,
    image,
    send_sem,
    recv_sem,
    hsend_sem,
    hrecv_sem,
):
    n = n_slab * n_side
    slab = lax.axis_index("slab")
    side = lax.axis_index("side")
    me = slab * n_side + side
    depth, width, span = pop.shape[1:]
    points = cell.shape[1]
    nblocks = n * SUB
    hist = rhist.shape[0]

    def dev(index):
        return {"slab": index // n_side, "side": index % n_side}

    barrier = pltpu.get_barrier_semaphore()

    def greet(o, carry):
        pl.semaphore_signal(barrier, inc=1, device_id=dev((me + o) % n), device_id_type=MESH)
        return carry

    lax.fori_loop(1, n, greet, 0)

    for hi in range(SUB):
        nbuf[me, :, hi, :] = nodes[:, hi * 128 : (hi + 1) * 128]
        spb[:, hi, :] = sprev[:, hi * 128 : (hi + 1) * 128]
    pl.semaphore_wait(barrier, n - 1)

    def exchange(stage, source, target):
        def one(o, carry):
            peer = (me + o) % n
            pltpu.make_async_remote_copy(
                src_ref=source(peer),
                dst_ref=target.at[me],
                send_sem=send_sem.at[stage, peer],
                recv_sem=recv_sem.at[stage, me],
                device_id=dev(peer),
                device_id_type=MESH,
            ).start()
            return carry

        lax.fori_loop(1, n, one, 0)

    def arrived(stage, target):
        def one(o, carry):
            peer = (me + o) % n
            pltpu.make_async_remote_copy(
                src_ref=target.at[peer],
                dst_ref=target.at[peer],
                send_sem=send_sem.at[stage, peer],
                recv_sem=recv_sem.at[stage, peer],
                device_id=dev(peer),
                device_id_type=MESH,
            ).wait_recv()
            return carry

        lax.fori_loop(1, n, one, 0)

    def departed(stage, source):
        def one(o, carry):
            peer = (me + o) % n
            pltpu.make_async_remote_copy(
                src_ref=source(peer),
                dst_ref=source(peer),
                send_sem=send_sem.at[stage, peer],
                recv_sem=recv_sem.at[stage, peer],
                device_id=dev(peer),
                device_id_type=MESH,
            ).wait_send()
            return carry

        lax.fori_loop(1, n, one, 0)

    exchange(0, lambda peer: nbuf.at[me], nbuf)

    chunks = width // 8

    def collide(i, carry):
        z = i // chunks
        x = pl.multiple_of((i % chunks) * 8, 8)
        xp = pl.multiple_of((i % chunks) * 8 + PAD, 8)
        f = [pop[d, z, pl.ds(x, 8), :] for d in range(19)]
        solid = mask[z, pl.ds(x, 8), :] == 1
        density = f[0]
        mom = [None, None, None]
        for d in range(1, 19, 2):
            density = density + (f[d] + f[d + 1])
            diff = f[d] - f[d + 1]
            for axis in range(3):
                c = int(velocities[d, axis])
                if c:
                    if mom[axis] is None:
                        mom[axis] = diff if c > 0 else -diff
                    else:
                        mom[axis] = mom[axis] + diff if c > 0 else mom[axis] - diff
        inv = 1.0 / density
        u = [m * inv for m in mom]
        base = 1.0 - 1.5 * (u[0] * u[0] + u[1] * u[1] + u[2] * u[2])
        keep = 1.0 - relax_rate
        weighted = density * (relax_rate * lattice_weights[0])
        padded[0, z + 1, pl.ds(xp, 8), :] = jnp.where(solid, f[0], keep * f[0] + weighted * base)
        scaled = {w: density * (relax_rate * w) for w in (1.0 / 18.0, 1.0 / 36.0)}
        for d in range(1, 19, 2):
            project = None
            for axis in range(3):
                c = int(velocities[d, axis])
                if c:
                    if project is None:
                        project = u[axis] if c > 0 else -u[axis]
                    else:
                        project = project + u[axis] if c > 0 else project - u[axis]
            w = scaled[lattice_weights[d]]
            even = w * (base + 4.5 * project * project)
            odd = w * (3.0 * project)
            padded[d, z + 1, pl.ds(xp, 8), :] = jnp.where(
                solid, f[d + 1], keep * f[d] + (even + odd)
            )
            padded[d + 1, z + 1, pl.ds(xp, 8), :] = jnp.where(
                solid, f[d], keep * f[d + 1] + (even - odd)
            )
        return carry

    lax.fori_loop(0, depth * chunks, collide, 0)

    halos = []
    for slot, s in enumerate((1, -1)):
        plane = depth if s > 0 else 1
        for j, d in enumerate(z_dirs[s]):
            zsend[slot, j] = padded[d, plane, PAD : PAD + width, :]
        place = {"slab": (slab + s + n_slab) % n_slab}
        halos.append((zsend.at[slot], zrecv.at[slot], slot, place))
    for slot, s in enumerate((1, -1)):
        row = PAD + width - 1 if s > 0 else PAD
        for j, d in enumerate(x_dirs[s]):
            for z in range(depth):
                xsend[slot, j, z : z + 1, :] = padded[d, 1 + z, row : row + 1, :]
        place = {"side": (side + s + n_side) % n_side}
        halos.append((xsend.at[slot], xrecv.at[slot], 2 + slot, place))
    for slot, (d, sx, sz) in enumerate(corners):
        plane = depth if sz > 0 else 1
        row = PAD + width - 1 if sx > 0 else PAD
        csend[slot] = jnp.broadcast_to(padded[d, plane, row : row + 1, :], (8, span))
        place = {
            "slab": (slab + sz + n_slab) % n_slab,
            "side": (side + sx + n_side) % n_side,
        }
        halos.append((csend.at[slot], crecv.at[slot], 4 + slot, place))
    halo_copies = []
    for source, target, index, place in halos:
        copy = pltpu.make_async_remote_copy(
            src_ref=source,
            dst_ref=target,
            send_sem=hsend_sem.at[index],
            recv_sem=hrecv_sem.at[index],
            device_id=place,
            device_id_type=MESH,
        )
        copy.start()
        halo_copies.append(copy)

    elems = enodes.shape[1]
    prev_pieces = stacked_pieces(spb[...].reshape(3 * SUB, 128), 3)
    rows = 3 * SUB
    for c in range(4):
        ids = enodes[c : c + 1, :]
        low = onehot(ids & 127, 128).astype(bf16)
        high = rows_iota(SUB, elems) == (ids >> 7)
        got = mm(prev_pieces, low)
        got = got[0:rows] + got[rows : 2 * rows] + got[2 * rows : 3 * rows]
        for k in range(3):
            part = jnp.where(high, got[k * SUB : (k + 1) * SUB], 0.0)
            dofs[3 * c + k : 3 * c + k + 1, :] = jnp.sum(part, axis=0, keepdims=True)
    local = dofs[...]
    for i in range(12):
        force[i : i + 1, :] = jnp.sum(stiff[i] * local, axis=0, keepdims=True)
    total = jnp.zeros((3 * rows, 128), f32)
    for c in range(4):
        ids = enodes[c : c + 1, :]
        low = onehot(ids & 127, 128).astype(bf16)
        high = rows_iota(SUB, elems) == (ids >> 7)
        spread = [jnp.where(high, force[3 * c + k : 3 * c + k + 1, :], 0.0) for k in range(3)]
        total = total + mm_nt(stacked_pieces(jnp.concatenate(spread, axis=0), 3), low)
    total = total[0:rows] + total[rows : 2 * rows] + total[2 * rows : 3 * rows]
    stiffed[...] = total.reshape(3, SUB, 128)

    def row_of(i, j):
        return sum(hist + 1 - q for q in range(i)) + (j - i)

    pairs = row_of(hist, hist) + 1
    gbuf[me] = jnp.zeros(gbuf.shape[1:], f32)
    for i in range(hist):
        for j in range(i, hist):
            r = row_of(i + 1, j + 1)
            gbuf[me, r : r + 1, :] = fold_lanes(rhist[i] * rhist[j])

    arrived(0, nbuf)
    step = 512 if nblocks <= 128 else 128
    node_pieces = []
    for k in range(3):
        turned = nbuf[:, k].reshape(nblocks, BLOCK).T
        node_pieces.append(jnp.concatenate(pieces(turned, 3), axis=1))
    wide[...] = jnp.concatenate(node_pieces, axis=0)

    def group_of(at):
        return owner[:, pl.ds(at, step)] * SUB + block[:, pl.ds(at, step)]

    def weigh(i, carry):
        at = pl.multiple_of(i * step, step)
        hot = onehot(group_of(at), nblocks).astype(bf16)
        support = mm(wide[...], jnp.concatenate([hot, hot, hot], axis=0))
        distance = None
        for k in range(3):
            offset = support[k * BLOCK : (k + 1) * BLOCK] - coords[k : k + 1, pl.ds(at, step)]
            square = offset * offset
            distance = square if distance is None else distance + square
        phi = 1.0 / (1.0 + distance * (1.0 / support_scale))
        weight = phi * (1.0 / jnp.sum(phi, axis=0, keepdims=True))
        upper, lower = pieces(weight, 2)
        whi[:, pl.ds(at, step)] = upper
        wlo[:, pl.ds(at, step)] = lower
        return carry

    lax.fori_loop(0, points // step, weigh, 0)

    for copy in halo_copies:
        copy.wait_recv()
    for slot, s in enumerate((1, -1)):
        plane = 0 if s > 0 else depth + 1
        for j, d in enumerate(z_dirs[s]):
            padded[d, plane, PAD : PAD + width, :] = zrecv[slot, j]
    for slot, s in enumerate((1, -1)):
        row = PAD - 1 if s > 0 else PAD + width
        for j, d in enumerate(x_dirs[s]):
            for z in range(depth):
                padded[d, 1 + z, row : row + 1, :] = xrecv[slot, j, z : z + 1, :]
    for slot, (d, sx, sz) in enumerate(corners):
        plane = 0 if sz > 0 else depth + 1
        row = PAD - 1 if sx > 0 else PAD + width
        padded[d, plane, row : row + 1, :] = crecv[slot, 0:1, :]

    def stream(z, carry):
        for x in range(0, width, 16):
            density = None
            mom = [None, None, None]
            for d in range(19):
                cx, cy, cz = (int(v) for v in velocities[d])
                piece = padded[d, z + 1 - cz, PAD + x - cx : PAD + x - cx + 16, :]
                if cy:
                    piece = pltpu.roll(piece, cy % span, 1)
                out_pop[d, z, x : x + 16, :] = piece
                density = piece if density is None else density + piece
                for axis, c in enumerate((cx, cy, cz)):
                    if c:
                        if mom[axis] is None:
                            mom[axis] = piece if c > 0 else -piece
                        else:
                            mom[axis] = mom[axis] + piece if c > 0 else mom[axis] - piece
            where = pl.ds(pl.multiple_of(z * width + x, 16), 16)
            fields[0, where, :] = (density - base_density) * (1.0 / 3.0)
            for axis in range(3):
                fields[1 + axis, where, :] = mom[axis]
        return carry

    lax.fori_loop(0, depth, stream, 0)

    cells = depth * width
    turned = jnp.concatenate([fields[k].T for k in range(4)], axis=0)
    turned_hi, turned_lo = pieces(turned, 2)
    tstep = 512

    def sample(i, carry):
        at = pl.multiple_of(i * tstep, tstep)
        ids = cell[:, pl.ds(at, tstep)]
        hot = onehot(ids // span, cells).astype(bf16)
        picked = mm(turned_hi, hot) + mm(turned_lo, hot)
        chosen = rows_iota(span, tstep) == (ids % span)
        got = []
        for k in range(4):
            part = jnp.where(chosen, picked[k * span : (k + 1) * span], 0.0)
            got.append(jnp.sum(part, axis=0, keepdims=True))
        for k in range(3):
            tract[k : k + 1, pl.ds(at, tstep)] = (
                got[0] * normal[k : k + 1, pl.ds(at, tstep)] + got[1 + k]
            )
        return carry

    lax.fori_loop(0, points // tstep, sample, 0)

    def gather_load(i, total):
        at = pl.multiple_of(i * step, step)
        chosen = rows_iota(nblocks, step) == group_of(at)
        spread = [jnp.where(chosen, tract[k : k + 1, pl.ds(at, step)], 0.0) for k in range(3)]
        upper, lower = pieces(jnp.concatenate(spread, axis=0), 2)
        first, second = whi[:, pl.ds(at, step)], wlo[:, pl.ds(at, step)]
        return total + (mm_nt(upper, first) + (mm_nt(lower, first) + mm_nt(upper, second)))

    load = lax.fori_loop(
        0, points // step, gather_load, jnp.zeros((3 * nblocks, BLOCK), f32)
    )
    for k in range(3):
        lsend[:, k] = load[k * nblocks : (k + 1) * nblocks].reshape(n, SUB, BLOCK)
    exchange(1, lambda peer: lsend.at[peer], lrecv)
    lrecv[me] = lsend[me]
    arrived(1, lrecv)
    load = jnp.sum(lrecv[...], axis=0)

    disp = spb[...] + comp[...][None] * (load - stiffed[...])
    dbuf[me] = disp
    exchange(2, lambda peer: dbuf.at[me], dbuf)
    for hi in range(SUB):
        out_disp[:, hi * 128 : (hi + 1) * 128] = dbuf[me, :, hi, :]
    arrived(2, dbuf)

    field = jnp.concatenate([dbuf[:, k].reshape(nblocks, BLOCK) for k in range(3)], axis=0)
    field_hi, field_lo = pieces(field, 2)

    def map_back(i, carry):
        at = pl.multiple_of(i * step, step)
        first, second = whi[:, pl.ds(at, step)], wlo[:, pl.ds(at, step)]
        mapped = mm(field_hi, first) + (mm(field_lo, first) + mm(field_hi, second))
        chosen = rows_iota(nblocks, step) == group_of(at)
        for k in range(3):
            part = jnp.where(chosen, mapped[k * nblocks : (k + 1) * nblocks], 0.0)
            image[k : k + 1, pl.ds(at, step)] = jnp.sum(part, axis=0, keepdims=True)
        return carry

    lax.fori_loop(0, points // step, map_back, 0)

    resid = image[...] - iterate[...]
    fresh = resid - rprev[...]
    gbuf[me, 0:1, :] = fold_lanes(fresh * fresh)
    gbuf[me, pairs : pairs + 1, :] = fold_lanes(fresh * resid)
    for i in range(hist):
        r = row_of(0, i + 1)
        gbuf[me, r : r + 1, :] = fold_lanes(fresh * rhist[i])
        gbuf[me, pairs + 1 + i : pairs + 2 + i, :] = fold_lanes(resid * rhist[i])
    exchange(3, lambda peer: gbuf.at[me], gbuf)
    arrived(3, gbuf)
    sums = jnp.sum(jnp.sum(gbuf[...], axis=0), axis=1, keepdims=True)
    size = hist + 1

    def entry(r):
        return sums[r : r + 1, 0:1]

    matrix = [[entry(row_of(min(i, j), max(i, j))) for j in range(size)] for i in range(size)]
    rhs = [-entry(pairs + i) for i in range(size)]
    for pivot in range(size):
        scale = 1.0 / matrix[pivot][pivot]
        row_vals = [v * scale for v in matrix[pivot]]
        value = rhs[pivot] * scale
        for i in range(size):
            if i != pivot:
                factor = matrix[i][pivot]
                matrix[i] = [matrix[i][j] - factor * row_vals[j] for j in range(size)]
                rhs[i] = rhs[i] - factor * value
        matrix[pivot], rhs[pivot] = row_vals, value
    result = image[...] + rhs[0] * (image[...] - iprev[...])
    for i in range(hist):
        result = result + rhs[1 + i] * ihist[i]
    out_iter[...] = result

    for copy in halo_copies:
        copy.wait_send()
    departed(0, lambda peer: nbuf.at[me])
    departed(1, lambda peer: lsend.at[peer])
    departed(2, lambda peer: dbuf.at[me])
    departed(3, lambda peer: gbuf.at[me])


def body(n_slab, n_side, *args):
    (
        populations,
        solid_mask,
        point_cell,
        point_owner,
        point_block,
        point_coords,
        point_normal,
        node_coords,
        struct_prev,
        compliance,
        elem_nodes,
        elem_stiff,
        iterate,
        resid_prev,
        image_prev,
        resid_history,
        image_history,
    ) = args
    n = n_slab * n_side
    directions, depth, width, span = populations.shape
    points = point_cell.shape[0]
    elems = elem_nodes.shape[1]
    nblocks = n * SUB
    vmem = pl.BlockSpec(memory_space=pltpu.VMEM)
    DMA = pltpu.SemaphoreType.DMA
    return pl.pallas_call(
        functools.partial(kernel, n_slab, n_side),
        out_shape=(
            jax.ShapeDtypeStruct(populations.shape, f32),
            jax.ShapeDtypeStruct(struct_prev.shape, f32),
            jax.ShapeDtypeStruct(iterate.shape, f32),
        ),
        in_specs=[vmem] * 17,
        out_specs=(vmem, vmem, vmem),
        scratch_shapes=[
            pltpu.VMEM((directions, depth + 2, width + 2 * PAD, span), f32),
            pltpu.VMEM((4, depth * width, span), f32),
            pltpu.VMEM((2, 5, width, span), f32),
            pltpu.VMEM((2, 5, width, span), f32),
            pltpu.VMEM((2, 5, depth, span), f32),
            pltpu.VMEM((2, 5, depth, span), f32),
            pltpu.VMEM((4, 8, span), f32),
            pltpu.VMEM((4, 8, span), f32),
            pltpu.VMEM((n, 3, SUB, BLOCK), f32),
            pltpu.VMEM((n, 3, SUB, BLOCK), f32),
            pltpu.VMEM((n, 3, SUB, BLOCK), f32),
            pltpu.VMEM((n, 3, SUB, BLOCK), f32),
            pltpu.VMEM((n, 24, BLOCK), f32),
            pltpu.VMEM((3 * BLOCK, 3 * nblocks), bf16),
            pltpu.VMEM((3, SUB, BLOCK), f32),
            pltpu.VMEM((12, elems), f32),
            pltpu.VMEM((12, elems), f32),
            pltpu.VMEM((3, SUB, BLOCK), f32),
            pltpu.VMEM((BLOCK, points), bf16),
            pltpu.VMEM((BLOCK, points), bf16),
            pltpu.VMEM((3, points), f32),
            pltpu.VMEM((3, points), f32),
            DMA((4, n)),
            DMA((4, n)),
            DMA((HALO_SLOTS,)),
            DMA((HALO_SLOTS,)),
        ],
        compiler_params=pltpu.CompilerParams(
            collective_id=0, has_side_effects=True, vmem_limit_bytes=52 * 2**20
        ),
    )(
        populations,
        solid_mask,
        point_cell.reshape(1, points),
        point_owner.reshape(1, points),
        point_block.reshape(1, points),
        point_coords,
        point_normal,
        node_coords,
        struct_prev,
        compliance.reshape(SUB, BLOCK),
        elem_nodes,
        elem_stiff,
        iterate,
        resid_prev,
        image_prev,
        resid_history,
        image_history,
    )


def solution(mesh):
    lattice = P(None, ("groups", "slab"), "side", None)
    last = P(None, ("groups", "slab", "side"))
    one = P(("groups", "slab", "side"))
    deep = P(None, None, ("groups", "slab", "side"))
    return jax.shard_map(
        functools.partial(body, mesh.shape["slab"], mesh.shape["side"]),
        mesh=mesh,
        in_specs=(
            P(None, ("groups", "slab"), "side", None),
            P(("groups", "slab"), "side", None),
            one,
            P(("groups", "slab", "side"), None),
            one,
            last,
            last,
            last,
            last,
            one,
            last,
            deep,
            last,
            last,
            last,
            deep,
            deep,
        ),
        out_specs=(lattice, last, last),
        check_vma=False,
    )
```

profile of v0, /device:TPU:0, one launch (start us, length us, event | category | flops | bytes accessed | tf_op | source)
XLA Modules:
  0.0 67.0 jit_solution(16591419505103197214)
XLA Ops:
  0.6 1.0 %copy.20.rhist = f32[4,3,2048]{2,1,0:T(4,128)S(1)} copy(f32[4,3,2048]{2,0,1:T(4,128)} %param.32) | data formatting | bytes 196608 | tf_op args[15]
  1.6 1.0 %copy.21.ihist = f32[4,3,2048]{2,1,0:T(4,128)S(1)} copy(f32[4,3,2048]{2,0,1:T(4,128)} %param.33) | data formatting | bytes 196608 | tf_op args[16]
  2.6 0.0 copy-start
  2.6 1.1 %copy-done = f32[12,12,1024]{2,1,0:T(8,128)S(1)} copy-done((f32[12,12,1024]{2,1,0:T(8,128)S(1)}, f32[12,12,1024]{2,1,0:T(8,128)}, u32[]{:S(2)}) %copy-start) | copy-done | bytes 589848
  3.7 0.0 copy-start.1
  3.7 0.9 %copy-done.1 = s32[4,64,128]{2,1,0:T(8,128)S(1)} copy-done((s32[4,64,128]{2,1,0:T(8,128)S(1)}, s32[4,64,128]{2,1,0:T(8,128)}, u32[]{:S(2)}) %copy-start.1) | copy-done | bytes 131096
  4.6 0.0 copy-start.2
  4.6 0.8 %copy-done.2 = f32[3,2048]{1,0:T(4,128)S(1)} copy-done((f32[3,2048]{1,0:T(4,128)S(1)}, f32[3,2048]{1,0:T(4,128)}, u32[]{:S(2)}) %copy-start.2) | copy-done | bytes 24600
  5.4 0.0 copy-start.3
  5.4 0.8 %copy-done.3 = f32[3,2048]{1,0:T(4,128)S(1)} copy-done((f32[3,2048]{1,0:T(4,128)S(1)}, f32[3,2048]{1,0:T(4,128)}, u32[]{:S(2)}) %copy-start.3) | copy-done | bytes 24600
  6.1 0.0 copy-start.4
  6.1 0.8 %copy-done.4 = f32[3,2048]{1,0:T(4,128)S(1)} copy-done((f32[3,2048]{1,0:T(4,128)S(1)}, f32[3,2048]{1,0:T(4,128)}, u32[]{:S(2)}) %copy-start.4) | copy-done | bytes 24600
  6.9 0.0 copy-start.5
  6.9 0.8 %copy-done.5 = f32[3,2048]{1,0:T(4,128)S(1)} copy-done((f32[3,2048]{1,0:T(4,128)S(1)}, f32[3,2048]{1,0:T(4,128)}, u32[]{:S(2)}) %copy-start.5) | copy-done | bytes 24600
  7.6 0.0 copy-start.6
  7.6 0.8 %copy-done.6 = f32[3,2048]{1,0:T(4,128)S(1)} copy-done((f32[3,2048]{1,0:T(4,128)S(1)}, f32[3,2048]{1,0:T(4,128)}, u32[]{:S(2)}) %copy-start.6) | copy-done | bytes 24600
  8.4 0.0 copy-start.7
  8.4 0.7 %copy-done.7 = f32[3,1024]{1,0:T(4,128)S(1)} copy-done((f32[3,1024]{1,0:T(4,128)S(1)}, f32[3,1024]{1,0:T(4,128)}, u32[]{:S(2)}) %copy-start.7) | copy-done | bytes 12312
  9.1 0.0 copy-start.8
  9.1 0.7 %copy-done.8 = f32[3,1024]{1,0:T(4,128)S(1)} copy-done((f32[3,1024]{1,0:T(4,128)S(1)}, f32[3,1024]{1,0:T(4,128)}, u32[]{:S(2)}) %copy-start.8) | copy-done | bytes 12312
  9.8 0.0 copy-start.9
  9.8 0.7 %copy-done.9 = s32[4,1024]{1,0:T(4,128)S(1)} copy-done((s32[4,1024]{1,0:T(4,128)S(1)}, s32[4,1024]{1,0:T(4,128)}, u32[]{:S(2)}) %copy-start.9) | copy-done | bytes 16408
  10.6 0.0 copy-start.10
  10.6 0.7 %copy-done.10 = s32[2048]{0:T(1024)S(1)} copy-done((s32[2048]{0:T(1024)S(1)}, s32[2048]{0:T(1024)}, u32[]{:S(2)}) %copy-start.10) | copy-done | bytes 8216
  11.2 0.0 copy-start.11
  11.2 0.7 %copy-done.11 = s32[2048,1]{0,1:T(1,128)S(1)} copy-done((s32[2048,1]{0,1:T(1,128)S(1)}, s32[2048,1]{0,1:T(1,128)}, u32[]{:S(2)}) %copy-start.11) | copy-done | bytes 8216
  11.9 0.7 %copy-done.12 = s32[2048]{0:T(1024)S(1)} copy-done((s32[2048]{0:T(1024)S(1)}, s32[2048]{0:T(1024)}, u32[]{:S(2)}) %copy-start.12) | copy-done | bytes 8216
  12.6 0.7 %copy-done.13 = f32[1024]{0:T(1024)S(1)} copy-done((f32[1024]{0:T(1024)S(1)}, f32[1024]{0:T(1024)}, u32[]{:S(2)}) %copy-start.13) | copy-done | bytes 4120
  13.3 49.0 %shard_map.184 = (f32[19,4,64,128]{3,2,1,0:T(8,128)}, f32[3,1024]{1,0:T(4,128)S(1)}, f32[3,2048]{1,0:T(4,128)S(1)}) custom-call(f32[19,4,64,128]{3,2,1,0:T(8,128)} %pop.1, s32[4,64,128]{2,1,0:T(8,128)S(1)} %copy-done.1, s32[1,2048]{1,0:T(1,128)S(1)} %bitcast.4, s32[1,2048]{1,0:T(1,128)S(1)} %bitcast.5, s32[1,2048]{1,0:T(1,128)S(1)} %bitcast.6, ...), custom_call_target="tpu_custom_call" | custom-call | tf_op jit(solution)/shard_map/pallas_call | solution.py:541
  62.3 3.5 %copy.25 = f32[19,4,64,128]{3,2,1,0:T(8,128)} copy(f32[19,4,64,128]{3,2,1,0:T(8,128)} %get-tuple-element.6) | data formatting | bytes 4980736
  65.8 0.6 copy.26
  66.4 0.6 copy.27
  (2 shorter events, 0.0 us)
Async XLA Ops:
  2.6 1.1 %copy-start = (f32[12,12,1024]{2,1,0:T(8,128)S(1)}, f32[12,12,1024]{2,1,0:T(8,128)}, u32[]{:S(2)}) copy-start(f32[12,12,1024]{2,1,0:T(8,128)} %stiff.1) | copy-start | bytes 1769476
  3.7 0.9 %copy-start.1 = (s32[4,64,128]{2,1,0:T(8,128)S(1)}, s32[4,64,128]{2,1,0:T(8,128)}, u32[]{:S(2)}) copy-start(s32[4,64,128]{2,1,0:T(8,128)} %mask.1) | copy-start | bytes 393220
  4.6 0.8 %copy-start.2 = (f32[3,2048]{1,0:T(4,128)S(1)}, f32[3,2048]{1,0:T(4,128)}, u32[]{:S(2)}) copy-start(f32[3,2048]{1,0:T(4,128)} %coords.1) | copy-start | bytes 73732
  5.4 0.8 %copy-start.3 = (f32[3,2048]{1,0:T(4,128)S(1)}, f32[3,2048]{1,0:T(4,128)}, u32[]{:S(2)}) copy-start(f32[3,2048]{1,0:T(4,128)} %normal.1) | copy-start | bytes 73732
  6.1 0.8 %copy-start.4 = (f32[3,2048]{1,0:T(4,128)S(1)}, f32[3,2048]{1,0:T(4,128)}, u32[]{:S(2)}) copy-start(f32[3,2048]{1,0:T(4,128)} %iterate.1) | copy-start | bytes 73732
  6.9 0.8 %copy-start.5 = (f32[3,2048]{1,0:T(4,128)S(1)}, f32[3,2048]{1,0:T(4,128)}, u32[]{:S(2)}) copy-start(f32[3,2048]{1,0:T(4,128)} %rprev.1) | copy-start | bytes 73732
  7.6 0.8 %copy-start.6 = (f32[3,2048]{1,0:T(4,128)S(1)}, f32[3,2048]{1,0:T(4,128)}, u32[]{:S(2)}) copy-start(f32[3,2048]{1,0:T(4,128)} %iprev.1) | copy-start | bytes 73732
  8.4 0.7 %copy-start.7 = (f32[3,1024]{1,0:T(4,128)S(1)}, f32[3,1024]{1,0:T(4,128)}, u32[]{:S(2)}) copy-start(f32[3,1024]{1,0:T(4,128)} %nodes.1) | copy-start | bytes 36868
  9.1 0.7 %copy-start.8 = (f32[3,1024]{1,0:T(4,128)S(1)}, f32[3,1024]{1,0:T(4,128)}, u32[]{:S(2)}) copy-start(f32[3,1024]{1,0:T(4,128)} %sprev.1) | copy-start | bytes 36868
  9.8 0.7 %copy-start.9 = (s32[4,1024]{1,0:T(4,128)S(1)}, s32[4,1024]{1,0:T(4,128)}, u32[]{:S(2)}) copy-start(s32[4,1024]{1,0:T(4,128)} %enodes.1) | copy-start | bytes 49156
  10.6 0.7 %copy-start.10 = (s32[2048]{0:T(1024)S(1)}, s32[2048]{0:T(1024)}, u32[]{:S(2)}) copy-start(s32[2048]{0:T(1024)} %param.19) | copy-start | bytes 24580
  11.2 0.7 %copy-start.11 = (s32[2048,1]{0,1:T(1,128)S(1)}, s32[2048,1]{0,1:T(1,128)}, u32[]{:S(2)}) copy-start(s32[2048,1]{0,1:T(1,128)} %param.20) | copy-start | bytes 24580
  11.9 0.7 %copy-start.12 = (s32[2048]{0:T(1024)S(1)}, s32[2048]{0:T(1024)}, u32[]{:S(2)}) copy-start(s32[2048]{0:T(1024)} %param.21) | copy-start | bytes 24580
  12.6 0.7 %copy-start.13 = (f32[1024]{0:T(1024)S(1)}, f32[1024]{0:T(1024)}, u32[]{:S(2)}) copy-start(f32[1024]{0:T(1024)} %param.26) | copy-start | bytes 12292
where the time goes:
time: 67.9 us; the launch traced here: 67 us
  Pallas kernels  49 us (72%)
  local copies, waits for them, and re-layouts  17.4 us (26%)
    pallas_call x1, Pallas kernels, body(): pl.pallas_call(functools.partial(kernel, n_slab, n_side), out_shape=(jax....  49 us
    unnamed x33, local copies, waits for them, and re-layouts  17.4 us

commit v1 on v0

--- a/solution.py
+++ b/solution.py
@@ -98,23 +98,23 @@
 def kernel(
     n_slab,
     n_side,
-    pop,
-    mask,
-    cell,
-    owner,
-    block,
-    coords,
-    normal,
-    nodes,
-    sprev,
-    comp,
-    enodes,
-    stiff,
-    iterate,
-    rprev,
-    iprev,
-    rhist,
-    ihist,
+    pop_in,
+    mask_in,
+    cell_in,
+    owner_in,
+    block_in,
+    coords_in,
+    normal_in,
+    nodes_in,
+    sprev_in,
+    comp_in,
+    enodes_in,
+    stiff_in,
+    iterate_in,
+    rprev_in,
+    iprev_in,
+    rhist_in,
+    ihist_in,
     out_pop,
     out_disp,
     out_iter,
@@ -144,6 +144,26 @@
     recv_sem,
     hsend_sem,
     hrecv_sem,
+    vcols,
+    wcols,
+    load_sem,
+    pop,
+    mask,
+    cell,
+    owner,
+    block,
+    coords,
+    normal,
+    nodes,
+    sprev,
+    comp,
+    enodes,
+    stiff,
+    iterate,
+    rprev,
+    iprev,
+    rhist,
+    ihist,
 ):
     n = n_slab * n_side
     slab = lax.axis_index("slab")
@@ -152,7 +172,37 @@
     depth, width, span = pop.shape[1:]
     points = cell.shape[1]
     nblocks = n * SUB
-    hist = rhist.shape[0]
+    hist = rhist.shape[1]
+
+    order = ("nodes", "sprev", "pop", "mask", "enodes", "stiff", "owner", "block", "coords")
+    order += ("rhist", "ihist", "comp", "cell", "normal", "iterate", "rprev", "iprev")
+    held = dict(
+        pop=(pop_in, pop),
+        mask=(mask_in, mask),
+        cell=(cell_in, cell),
+        owner=(owner_in, owner),
+        block=(block_in, block),
+        coords=(coords_in, coords),
+        normal=(normal_in, normal),
+        nodes=(nodes_in, nodes),
+        sprev=(sprev_in, sprev),
+        comp=(comp_in, comp),
+        enodes=(enodes_in, enodes),
+        stiff=(stiff_in, stiff),
+        iterate=(iterate_in, iterate),
+        rprev=(rprev_in, rprev),
+        iprev=(iprev_in, iprev),
+        rhist=(rhist_in, rhist),
+        ihist=(ihist_in, ihist),
+    )
+    loads = {}
+    for place, name in enumerate(order):
+        loads[name] = pltpu.make_async_copy(*held[name], load_sem.at[place])
+        loads[name].start()
+
+    def ready(*names):
+        for name in names:
+            loads[name].wait()
 
     def dev(index):
         return {"slab": index // n_side, "side": index % n_side}
@@ -165,6 +215,7 @@
 
     lax.fori_loop(1, n, greet, 0)
 
+    ready("nodes", "sprev")
     for hi in range(SUB):
         nbuf[me, :, hi, :] = nodes[:, hi * 128 : (hi + 1) * 128]
         spb[:, hi, :] = sprev[:, hi * 128 : (hi + 1) * 128]
@@ -217,6 +268,7 @@
 
     exchange(0, lambda peer: nbuf.at[me], nbuf)
 
+    ready("pop", "mask")
     chunks = width // 8
 
     def collide(i, carry):
@@ -302,6 +354,7 @@
         copy.start()
         halo_copies.append(copy)
 
+    ready("enodes", "stiff")
     elems = enodes.shape[1]
     prev_pieces = stacked_pieces(spb[...].reshape(3 * SUB, 128), 3)
     rows = 3 * SUB
@@ -327,16 +380,14 @@
     total = total[0:rows] + total[rows : 2 * rows] + total[2 * rows : 3 * rows]
     stiffed[...] = total.reshape(3, SUB, 128)
 
-    def row_of(i, j):
-        return sum(hist + 1 - q for q in range(i)) + (j - i)
-
-    pairs = row_of(hist, hist) + 1
-    gbuf[me] = jnp.zeros(gbuf.shape[1:], f32)
-    for i in range(hist):
-        for j in range(i, hist):
-            r = row_of(i + 1, j + 1)
-            gbuf[me, r : r + 1, :] = fold_lanes(rhist[i] * rhist[j])
-
+    ready("rhist", "ihist")
+    for k in range(3):
+        vcols[k] = jnp.zeros(vcols.shape[1:], f32)
+        wcols[k] = jnp.zeros(wcols.shape[1:], f32)
+        vcols[k, 1 : 1 + hist, :] = rhist[k]
+        wcols[k, 1 : 1 + hist, :] = ihist[k]
+
+    ready("owner", "block", "coords")
     arrived(0, nbuf)
     step = 512 if nblocks <= 128 else 128
     node_pieces = []
@@ -407,6 +458,7 @@
 
     lax.fori_loop(0, depth, stream, 0)
 
+    ready("cell", "normal")
     cells = depth * width
     turned = jnp.concatenate([fields[k].T for k in range(4)], axis=0)
     turned_hi, turned_lo = pieces(turned, 2)
@@ -448,6 +500,7 @@
     arrived(1, lrecv)
     load = jnp.sum(lrecv[...], axis=0)
 
+    ready("comp")
     disp = spb[...] + comp[...][None] * (load - stiffed[...])
     dbuf[me] = disp
     exchange(2, lambda peer: dbuf.at[me], dbuf)
@@ -470,24 +523,27 @@
 
     lax.fori_loop(0, points // step, map_back, 0)
 
-    resid = image[...] - iterate[...]
-    fresh = resid - rprev[...]
-    gbuf[me, 0:1, :] = fold_lanes(fresh * fresh)
-    gbuf[me, pairs : pairs + 1, :] = fold_lanes(fresh * resid)
-    for i in range(hist):
-        r = row_of(0, i + 1)
-        gbuf[me, r : r + 1, :] = fold_lanes(fresh * rhist[i])
-        gbuf[me, pairs + 1 + i : pairs + 2 + i, :] = fold_lanes(resid * rhist[i])
+    ready("iterate", "rprev", "iprev")
+    gram = None
+    for k in range(3):
+        now = image[k : k + 1, :]
+        resid = now - iterate[k : k + 1, :]
+        vcols[k, 0:1, :] = resid - rprev[k : k + 1, :]
+        vcols[k, 1 + hist : 2 + hist, :] = resid
+        wcols[k, 0:1, :] = now - iprev[k : k + 1, :]
+        parts = stacked_pieces(vcols[k], 3)
+        term = mm_nt(parts, parts)
+        gram = term if gram is None else gram + term
+    gram = gram[0:8] + gram[8:16] + gram[16:24]
+    gram = gram[:, 0:8] + gram[:, 8:16] + gram[:, 16:24]
+    gbuf[me] = jnp.concatenate([gram, jnp.zeros((8, BLOCK - 8), f32)], axis=1)
     exchange(3, lambda peer: gbuf.at[me], gbuf)
     arrived(3, gbuf)
-    sums = jnp.sum(jnp.sum(gbuf[...], axis=0), axis=1, keepdims=True)
+    sums = jnp.sum(gbuf[...], axis=0)
     size = hist + 1
 
-    def entry(r):
-        return sums[r : r + 1, 0:1]
-
-    matrix = [[entry(row_of(min(i, j), max(i, j))) for j in range(size)] for i in range(size)]
-    rhs = [-entry(pairs + i) for i in range(size)]
+    matrix = [[sums[i : i + 1, j : j + 1] for j in range(size)] for i in range(size)]
+    rhs = [-sums[i : i + 1, size : size + 1] for i in range(size)]
     for pivot in range(size):
         scale = 1.0 / matrix[pivot][pivot]
         row_vals = [v * scale for v in matrix[pivot]]
@@ -498,10 +554,10 @@
                 matrix[i] = [matrix[i][j] - factor * row_vals[j] for j in range(size)]
                 rhs[i] = rhs[i] - factor * value
         matrix[pivot], rhs[pivot] = row_vals, value
-    result = image[...] + rhs[0] * (image[...] - iprev[...])
-    for i in range(hist):
-        result = result + rhs[1 + i] * ihist[i]
-    out_iter[...] = result
+    coeffs = jnp.concatenate(rhs + [jnp.zeros((8 - size, 1), f32)], axis=0)
+    for k in range(3):
+        change = jnp.sum(wcols[k] * coeffs, axis=0, keepdims=True)
+        out_iter[k : k + 1, :] = image[k : k + 1, :] + change
 
     for copy in halo_copies:
         copy.wait_send()
@@ -538,47 +594,7 @@
     nblocks = n * SUB
     vmem = pl.BlockSpec(memory_space=pltpu.VMEM)
     DMA = pltpu.SemaphoreType.DMA
-    return pl.pallas_call(
-        functools.partial(kernel, n_slab, n_side),
-        out_shape=(
-            jax.ShapeDtypeStruct(populations.shape, f32),
-            jax.ShapeDtypeStruct(struct_prev.shape, f32),
-            jax.ShapeDtypeStruct(iterate.shape, f32),
-        ),
-        in_specs=[vmem] * 17,
-        out_specs=(vmem, vmem, vmem),
-        scratch_shapes=[
-            pltpu.VMEM((directions, depth + 2, width + 2 * PAD, span), f32),
-            pltpu.VMEM((4, depth * width, span), f32),
-            pltpu.VMEM((2, 5, width, span), f32),
-            pltpu.VMEM((2, 5, width, span), f32),
-            pltpu.VMEM((2, 5, depth, span), f32),
-            pltpu.VMEM((2, 5, depth, span), f32),
-            pltpu.VMEM((4, 8, span), f32),
-            pltpu.VMEM((4, 8, span), f32),
-            pltpu.VMEM((n, 3, SUB, BLOCK), f32),
-            pltpu.VMEM((n, 3, SUB, BLOCK), f32),
-            pltpu.VMEM((n, 3, SUB, BLOCK), f32),
-            pltpu.VMEM((n, 3, SUB, BLOCK), f32),
-            pltpu.VMEM((n, 24, BLOCK), f32),
-            pltpu.VMEM((3 * BLOCK, 3 * nblocks), bf16),
-            pltpu.VMEM((3, SUB, BLOCK), f32),
-            pltpu.VMEM((12, elems), f32),
-            pltpu.VMEM((12, elems), f32),
-            pltpu.VMEM((3, SUB, BLOCK), f32),
-            pltpu.VMEM((BLOCK, points), bf16),
-            pltpu.VMEM((BLOCK, points), bf16),
-            pltpu.VMEM((3, points), f32),
-            pltpu.VMEM((3, points), f32),
-            DMA((4, n)),
-            DMA((4, n)),
-            DMA((HALO_SLOTS,)),
-            DMA((HALO_SLOTS,)),
-        ],
-        compiler_params=pltpu.CompilerParams(
-            collective_id=0, has_side_effects=True, vmem_limit_bytes=52 * 2**20
-        ),
-    )(
+    operands = (
         populations,
         solid_mask,
         point_cell.reshape(1, points),
@@ -594,9 +610,54 @@
         iterate,
         resid_prev,
         image_prev,
-        resid_history,
-        image_history,
+        resid_history.transpose(1, 0, 2),
+        image_history.transpose(1, 0, 2),
     )
+    return pl.pallas_call(
+        functools.partial(kernel, n_slab, n_side),
+        out_shape=(
+            jax.ShapeDtypeStruct(populations.shape, f32),
+            jax.ShapeDtypeStruct(struct_prev.shape, f32),
+            jax.ShapeDtypeStruct(iterate.shape, f32),
+        ),
+        in_specs=[pl.BlockSpec(memory_space=pltpu.HBM)] * len(operands),
+        out_specs=(vmem, vmem, vmem),
+        scratch_shapes=[
+            pltpu.VMEM((directions, depth + 2, width + 2 * PAD, span), f32),
+            pltpu.VMEM((4, depth * width, span), f32),
+            pltpu.VMEM((2, 5, width, span), f32),
+            pltpu.VMEM((2, 5, width, span), f32),
+            pltpu.VMEM((2, 5, depth, span), f32),
+            pltpu.VMEM((2, 5, depth, span), f32),
+            pltpu.VMEM((4, 8, span), f32),
+            pltpu.VMEM((4, 8, span), f32),
+            pltpu.VMEM((n, 3, SUB, BLOCK), f32),
+            pltpu.VMEM((n, 3, SUB, BLOCK), f32),
+            pltpu.VMEM((n, 3, SUB, BLOCK), f32),
+            pltpu.VMEM((n, 3, SUB, BLOCK), f32),
+            pltpu.VMEM((n, 8, BLOCK), f32),
+            pltpu.VMEM((3 * BLOCK, 3 * nblocks), bf16),
+            pltpu.VMEM((3, SUB, BLOCK), f32),
+            pltpu.VMEM((12, elems), f32),
+            pltpu.VMEM((12, elems), f32),
+            pltpu.VMEM((3, SUB, BLOCK), f32),
+            pltpu.VMEM((BLOCK, points), bf16),
+            pltpu.VMEM((BLOCK, points), bf16),
+            pltpu.VMEM((3, points), f32),
+            pltpu.VMEM((3, points), f32),
+            DMA((4, n)),
+            DMA((4, n)),
+            DMA((HALO_SLOTS,)),
+            DMA((HALO_SLOTS,)),
+            pltpu.VMEM((3, 8, points), f32),
+            pltpu.VMEM((3, 8, points), f32),
+            DMA((len(operands),)),
+        ]
+        + [pltpu.VMEM(x.shape, x.dtype) for x in operands],
+        compiler_params=pltpu.CompilerParams(
+            collective_id=0, has_side_effects=True, vmem_limit_bytes=63 * 2**20
+        ),
+    )(*operands)
 
 
 def solution(mesh):

time: 67.9 us -> 54 us (0.80); the launches traced: 67 us -> 53.8 us
  local copies, waits for them, and re-layouts: 17.4 us -> 4.7 us
    unnamed x33 -> x7, local copies, waits for them, and re-layouts: 17.4 us -> 4.7 us
where the time goes in v1:
time: 54 us; the launch traced here: 53.8 us
  Pallas kernels  48.4 us (90%)
  local copies, waits for them, and re-layouts  4.7 us (9%)
  between operations  0.66 us (1%)
    pallas_call x1, Pallas kernels, body(): pl.pallas_call(functools.partial(kernel, n_slab, n_side), out_shape=(jax....  48.4 us
    unnamed x7, local copies, waits for them, and re-layouts  4.7 us

profile of v1, /device:TPU:0, one launch (start us, length us, event | category | flops | bytes accessed | tf_op | source)
XLA Modules:
  0.0 53.8 jit_solution(5511914407806773998)
XLA Ops:
  0.6 48.4 %shard_map.184 = (f32[19,4,64,128]{3,2,1,0:T(8,128)}, f32[3,1024]{1,0:T(4,128)}, f32[3,2048]{1,0:T(4,128)}) custom-call(f32[19,4,64,128]{3,2,1,0:T(8,128)} %pop_in.1, s32[4,64,128]{2,1,0:T(8,128)} %mask_in.1, s32[1,2048]{1,0:T(1,128)} %bitcast.8, s32[1,2048]{1,0:T(1,128)} %bitcast.9, s32[1,2048]{1,0:T(1,128)} %bitcast.10, f32[3,2048]{1,0:T(4,128)} %coords_in.1, ...), custom_call_target="tpu_custom_call" | custom-call | tf_op jit(solution)/shard_map/pallas_call | solution.py:616
  49.1 0.0 copy-start.1
  49.1 0.0 copy-start
  49.1 3.5 %copy.23 = f32[19,4,64,128]{3,2,1,0:T(8,128)} copy(f32[19,4,64,128]{3,2,1,0:T(8,128)} %get-tuple-element.6) | data formatting | bytes 4980736
  52.5 0.0 copy-done.1
  52.5 0.6 %copy.24 = f32[3,1024]{1,0:T(4,128)} copy(f32[3,1024]{1,0:T(4,128)S(1)} %copy-done.1) | data formatting | bytes 24576
  53.2 0.0 copy-done
  53.2 0.6 %copy.25 = f32[3,2048]{1,0:T(4,128)} copy(f32[3,2048]{1,0:T(4,128)S(1)} %copy-done) | data formatting | bytes 49152
Async XLA Ops:
  49.1 3.5 %copy-start.1 = (f32[3,1024]{1,0:T(4,128)S(1)}, f32[3,1024]{1,0:T(4,128)}, u32[]{:S(2)}) copy-start(f32[3,1024]{1,0:T(4,128)} %get-tuple-element.7) | copy-start | bytes 36868
  49.1 4.1 %copy-start = (f32[3,2048]{1,0:T(4,128)S(1)}, f32[3,2048]{1,0:T(4,128)}, u32[]{:S(2)}) copy-start(f32[3,2048]{1,0:T(4,128)} %get-tuple-element.8) | copy-start | bytes 73732

commit v2 on v1

--- a/solution.py
+++ b/solution.py
@@ -147,6 +147,10 @@
     vcols,
     wcols,
     load_sem,
+    groups,
+    psend,
+    precv,
+    hbuf,
     pop,
     mask,
     cell,
@@ -168,7 +172,6 @@
     n = n_slab * n_side
     slab = lax.axis_index("slab")
     side = lax.axis_index("side")
-    me = slab * n_side + side
     depth, width, span = pop.shape[1:]
     points = cell.shape[1]
     nblocks = n * SUB
@@ -204,77 +207,77 @@
         for name in names:
             loads[name].wait()
 
-    def dev(index):
-        return {"slab": index // n_side, "side": index % n_side}
-
     barrier = pltpu.get_barrier_semaphore()
 
-    def greet(o, carry):
-        pl.semaphore_signal(barrier, inc=1, device_id=dev((me + o) % n), device_id_type=MESH)
-        return carry
-
-    lax.fori_loop(1, n, greet, 0)
+    extent = {"slab": (n_slab, slab), "side": (n_side, side)}
+
+    def partners(axis, act):
+        size, mine = extent[axis]
+
+        def one(o, carry):
+            act((mine + o) % size)
+            return carry
+
+        if size <= 4:
+            for o in range(1, size):
+                one(o, 0)
+        else:
+            lax.fori_loop(1, size, one, 0)
+
+    def greet(place):
+        pl.semaphore_signal(barrier, inc=1, device_id=place, device_id_type=MESH)
+
+    for axis in ("slab", "side"):
+        partners(axis, lambda peer: greet({axis: peer}))
+    for _, sx, sz in corners:
+        greet({"slab": (slab + sz + n_slab) % n_slab, "side": (side + sx + n_side) % n_side})
 
     ready("nodes", "sprev")
     for hi in range(SUB):
-        nbuf[me, :, hi, :] = nodes[:, hi * 128 : (hi + 1) * 128]
+        nbuf[side, slab, :, hi, :] = nodes[:, hi * 128 : (hi + 1) * 128]
         spb[:, hi, :] = sprev[:, hi * 128 : (hi + 1) * 128]
-    pl.semaphore_wait(barrier, n - 1)
-
-    def exchange(stage, source, target):
-        def one(o, carry):
-            peer = (me + o) % n
-            pltpu.make_async_remote_copy(
-                src_ref=source(peer),
-                dst_ref=target.at[me],
-                send_sem=send_sem.at[stage, peer],
-                recv_sem=recv_sem.at[stage, me],
-                device_id=dev(peer),
-                device_id_type=MESH,
-            ).start()
-            return carry
-
-        lax.fori_loop(1, n, one, 0)
-
-    def arrived(stage, target):
-        def one(o, carry):
-            peer = (me + o) % n
-            pltpu.make_async_remote_copy(
-                src_ref=target.at[peer],
-                dst_ref=target.at[peer],
-                send_sem=send_sem.at[stage, peer],
-                recv_sem=recv_sem.at[stage, peer],
-                device_id=dev(peer),
-                device_id_type=MESH,
-            ).wait_recv()
-            return carry
-
-        lax.fori_loop(1, n, one, 0)
-
-    def departed(stage, source):
-        def one(o, carry):
-            peer = (me + o) % n
-            pltpu.make_async_remote_copy(
-                src_ref=source(peer),
-                dst_ref=source(peer),
-                send_sem=send_sem.at[stage, peer],
-                recv_sem=recv_sem.at[stage, peer],
-                device_id=dev(peer),
-                device_id_type=MESH,
-            ).wait_send()
-            return carry
-
-        lax.fori_loop(1, n, one, 0)
-
-    exchange(0, lambda peer: nbuf.at[me], nbuf)
+    pl.semaphore_wait(barrier, n_slab + n_side - 2 + len(corners))
+
+    def transfer(stage, axis, peer, source, target, index):
+        return pltpu.make_async_remote_copy(
+            src_ref=source,
+            dst_ref=target,
+            send_sem=send_sem.at[stage, peer],
+            recv_sem=recv_sem.at[stage, index],
+            device_id={axis: peer},
+            device_id_type=MESH,
+        )
+
+    def exchange(stage, axis, source, target):
+        mine = extent[axis][1]
+        partners(
+            axis, lambda peer: transfer(stage, axis, peer, source(peer), target, mine).start()
+        )
+
+    def arrived(stage, axis, landing):
+        partners(
+            axis,
+            lambda peer: transfer(
+                stage, axis, peer, landing(peer), landing(peer), peer
+            ).wait_recv(),
+        )
+
+    def departed(stage, axis, source):
+        partners(
+            axis,
+            lambda peer: transfer(
+                stage, axis, peer, source(peer), source(peer), peer
+            ).wait_send(),
+        )
+
+    exchange(0, "slab", lambda peer: nbuf.at[side, slab], nbuf.at[side, slab])
 
     ready("pop", "mask")
     chunks = width // 8
 
-    def collide(i, carry):
-        z = i // chunks
-        x = pl.multiple_of((i % chunks) * 8, 8)
-        xp = pl.multiple_of((i % chunks) * 8 + PAD, 8)
+    def collide(z, i):
+        x = pl.multiple_of(i * 8, 8)
+        xp = pl.multiple_of(i * 8 + PAD, 8)
         f = [pop[d, z, pl.ds(x, 8), :] for d in range(19)]
         solid = mask[z, pl.ds(x, 8), :] == 1
         density = f[0]
@@ -314,35 +317,18 @@
             padded[d + 1, z + 1, pl.ds(xp, 8), :] = jnp.where(
                 solid, f[d], keep * f[d + 1] + (even - odd)
             )
+
+    def outer_planes(i, carry):
+        collide((i // chunks) * (depth - 1), i % chunks)
         return carry
 
-    lax.fori_loop(0, depth * chunks, collide, 0)
-
-    halos = []
-    for slot, s in enumerate((1, -1)):
-        plane = depth if s > 0 else 1
-        for j, d in enumerate(z_dirs[s]):
-            zsend[slot, j] = padded[d, plane, PAD : PAD + width, :]
-        place = {"slab": (slab + s + n_slab) % n_slab}
-        halos.append((zsend.at[slot], zrecv.at[slot], slot, place))
-    for slot, s in enumerate((1, -1)):
-        row = PAD + width - 1 if s > 0 else PAD
-        for j, d in enumerate(x_dirs[s]):
-            for z in range(depth):
-                xsend[slot, j, z : z + 1, :] = padded[d, 1 + z, row : row + 1, :]
-        place = {"side": (side + s + n_side) % n_side}
-        halos.append((xsend.at[slot], xrecv.at[slot], 2 + slot, place))
-    for slot, (d, sx, sz) in enumerate(corners):
-        plane = depth if sz > 0 else 1
-        row = PAD + width - 1 if sx > 0 else PAD
-        csend[slot] = jnp.broadcast_to(padded[d, plane, row : row + 1, :], (8, span))
-        place = {
-            "slab": (slab + sz + n_slab) % n_slab,
-            "side": (side + sx + n_side) % n_side,
-        }
-        halos.append((csend.at[slot], crecv.at[slot], 4 + slot, place))
+    def inner_planes(i, carry):
+        collide(1 + i // chunks, i % chunks)
+        return carry
+
     halo_copies = []
-    for source, target, index, place in halos:
+
+    def pass_halo(source, target, index, place):
         copy = pltpu.make_async_remote_copy(
             src_ref=source,
             dst_ref=target,
@@ -353,6 +339,33 @@
         )
         copy.start()
         halo_copies.append(copy)
+
+    lax.fori_loop(0, 2 * chunks, outer_planes, 0)
+    for slot, s in enumerate((1, -1)):
+        plane = depth if s > 0 else 1
+        for j, d in enumerate(z_dirs[s]):
+            zsend[slot, j] = padded[d, plane, PAD : PAD + width, :]
+        place = {"slab": (slab + s + n_slab) % n_slab}
+        pass_halo(zsend.at[slot], zrecv.at[slot], slot, place)
+    lax.fori_loop(0, (depth - 2) * chunks, inner_planes, 0)
+    for slot, s in enumerate((1, -1)):
+        row = PAD + width - 1 if s > 0 else PAD
+        for j, d in enumerate(x_dirs[s]):
+            for z in range(depth):
+                xsend[slot, j, z : z + 1, :] = padded[d, 1 + z, row : row + 1, :]
+        place = {"side": (side + s + n_side) % n_side}
+        pass_halo(xsend.at[slot], xrecv.at[slot], 2 + slot, place)
+    for slot, (d, sx, sz) in enumerate(corners):
+        plane = depth if sz > 0 else 1
+        row = PAD + width - 1 if sx > 0 else PAD
+        csend[slot] = jnp.broadcast_to(padded[d, plane, row : row + 1, :], (8, span))
+        place = {
+            "slab": (slab + sz + n_slab) % n_slab,
+            "side": (side + sx + n_side) % n_side,
+        }
+        pass_halo(csend.at[slot], crecv.at[slot], 4 + slot, place)
+    arrived(0, "slab", lambda peer: nbuf.at[side, peer])
+    exchange(1, "side", lambda peer: nbuf.at[side], nbuf.at[side])
 
     ready("enodes", "stiff")
     elems = enodes.shape[1]
@@ -388,16 +401,18 @@
         wcols[k, 1 : 1 + hist, :] = ihist[k]
 
     ready("owner", "block", "coords")
-    arrived(0, nbuf)
+    arrived(1, "side", lambda peer: nbuf.at[peer])
+    holder = owner[...]
+    groups[...] = ((holder % n_side) * n_slab + holder // n_side) * SUB + block[...]
     step = 512 if nblocks <= 128 else 128
     node_pieces = []
     for k in range(3):
-        turned = nbuf[:, k].reshape(nblocks, BLOCK).T
+        turned = nbuf[:, :, k].reshape(nblocks, BLOCK).T
         node_pieces.append(jnp.concatenate(pieces(turned, 3), axis=1))
     wide[...] = jnp.concatenate(node_pieces, axis=0)
 
     def group_of(at):
-        return owner[:, pl.ds(at, step)] * SUB + block[:, pl.ds(at, step)]
+        return groups[:, pl.ds(at, step)]
 
     def weigh(i, carry):
         at = pl.multiple_of(i * step, step)
@@ -494,21 +509,28 @@
         0, points // step, gather_load, jnp.zeros((3 * nblocks, BLOCK), f32)
     )
     for k in range(3):
-        lsend[:, k] = load[k * nblocks : (k + 1) * nblocks].reshape(n, SUB, BLOCK)
-    exchange(1, lambda peer: lsend.at[peer], lrecv)
-    lrecv[me] = lsend[me]
-    arrived(1, lrecv)
-    load = jnp.sum(lrecv[...], axis=0)
-
+        lsend[:, :, k] = load[k * nblocks : (k + 1) * nblocks].reshape(
+            n_side, n_slab, SUB, BLOCK
+        )
+    exchange(2, "side", lambda peer: lsend.at[peer], lrecv.at[side])
+    lrecv[side] = lsend[side]
     ready("comp")
+    arrived(2, "side", lambda peer: lrecv.at[peer])
+    psend[...] = jnp.sum(lrecv[...], axis=0)
+    exchange(3, "slab", lambda peer: psend.at[peer], precv.at[slab])
+    precv[slab] = psend[slab]
+    arrived(3, "slab", lambda peer: precv.at[peer])
+    load = jnp.sum(precv[...], axis=0)
     disp = spb[...] + comp[...][None] * (load - stiffed[...])
-    dbuf[me] = disp
-    exchange(2, lambda peer: dbuf.at[me], dbuf)
+    dbuf[side, slab] = disp
+    exchange(4, "slab", lambda peer: dbuf.at[side, slab], dbuf.at[side, slab])
     for hi in range(SUB):
-        out_disp[:, hi * 128 : (hi + 1) * 128] = dbuf[me, :, hi, :]
-    arrived(2, dbuf)
-
-    field = jnp.concatenate([dbuf[:, k].reshape(nblocks, BLOCK) for k in range(3)], axis=0)
+        out_disp[:, hi * 128 : (hi + 1) * 128] = dbuf[side, slab, :, hi, :]
+    arrived(4, "slab", lambda peer: dbuf.at[side, peer])
+    exchange(5, "side", lambda peer: dbuf.at[side], dbuf.at[side])
+    arrived(5, "side", lambda peer: dbuf.at[peer])
+
+    field = jnp.concatenate([dbuf[:, :, k].reshape(nblocks, BLOCK) for k in range(3)], axis=0)
     field_hi, field_lo = pieces(field, 2)
 
     def map_back(i, carry):
@@ -536,10 +558,13 @@
         gram = term if gram is None else gram + term
     gram = gram[0:8] + gram[8:16] + gram[16:24]
     gram = gram[:, 0:8] + gram[:, 8:16] + gram[:, 16:24]
-    gbuf[me] = jnp.concatenate([gram, jnp.zeros((8, BLOCK - 8), f32)], axis=1)
-    exchange(3, lambda peer: gbuf.at[me], gbuf)
-    arrived(3, gbuf)
-    sums = jnp.sum(gbuf[...], axis=0)
+    gbuf[side] = jnp.concatenate([gram, jnp.zeros((8, BLOCK - 8), f32)], axis=1)
+    exchange(6, "side", lambda peer: gbuf.at[side], gbuf.at[side])
+    arrived(6, "side", lambda peer: gbuf.at[peer])
+    hbuf[slab] = jnp.sum(gbuf[...], axis=0)
+    exchange(7, "slab", lambda peer: hbuf.at[slab], hbuf.at[slab])
+    arrived(7, "slab", lambda peer: hbuf.at[peer])
+    sums = jnp.sum(hbuf[...], axis=0)
     size = hist + 1
 
     matrix = [[sums[i : i + 1, j : j + 1] for j in range(size)] for i in range(size)]
@@ -561,10 +586,14 @@
 
     for copy in halo_copies:
         copy.wait_send()
-    departed(0, lambda peer: nbuf.at[me])
-    departed(1, lambda peer: lsend.at[peer])
-    departed(2, lambda peer: dbuf.at[me])
-    departed(3, lambda peer: gbuf.at[me])
+    departed(0, "slab", lambda peer: nbuf.at[side, slab])
+    departed(1, "side", lambda peer: nbuf.at[side])
+    departed(2, "side", lambda peer: lsend.at[peer])
+    departed(3, "slab", lambda peer: psend.at[peer])
+    departed(4, "slab", lambda peer: dbuf.at[side, slab])
+    departed(5, "side", lambda peer: dbuf.at[side])
+    departed(6, "side", lambda peer: gbuf.at[side])
+    departed(7, "slab", lambda peer: hbuf.at[slab])
 
 
 def body(n_slab, n_side, *args):
@@ -631,11 +660,11 @@
             pltpu.VMEM((2, 5, depth, span), f32),
             pltpu.VMEM((4, 8, span), f32),
             pltpu.VMEM((4, 8, span), f32),
-            pltpu.VMEM((n, 3, SUB, BLOCK), f32),
-            pltpu.VMEM((n, 3, SUB, BLOCK), f32),
-            pltpu.VMEM((n, 3, SUB, BLOCK), f32),
-            pltpu.VMEM((n, 3, SUB, BLOCK), f32),
-            pltpu.VMEM((n, 8, BLOCK), f32),
+            pltpu.VMEM((n_side, n_slab, 3, SUB, BLOCK), f32),
+            pltpu.VMEM((n_side, n_slab, 3, SUB, BLOCK), f32),
+            pltpu.VMEM((n_side, n_slab, 3, SUB, BLOCK), f32),
+            pltpu.VMEM((n_side, n_slab, 3, SUB, BLOCK), f32),
+            pltpu.VMEM((n_side, 8, BLOCK), f32),
             pltpu.VMEM((3 * BLOCK, 3 * nblocks), bf16),
             pltpu.VMEM((3, SUB, BLOCK), f32),
             pltpu.VMEM((12, elems), f32),
@@ -645,13 +674,17 @@
             pltpu.VMEM((BLOCK, points), bf16),
             pltpu.VMEM((3, points), f32),
             pltpu.VMEM((3, points), f32),
-            DMA((4, n)),
-            DMA((4, n)),
+            DMA((8, max(n_slab, n_side))),
+            DMA((8, max(n_slab, n_side))),
             DMA((HALO_SLOTS,)),
             DMA((HALO_SLOTS,)),
             pltpu.VMEM((3, 8, points), f32),
             pltpu.VMEM((3, 8, points), f32),
             DMA((len(operands),)),
+            pltpu.VMEM((1, points), jnp.int32),
+            pltpu.VMEM((n_slab, 3, SUB, BLOCK), f32),
+            pltpu.VMEM((n_slab, 3, SUB, BLOCK), f32),
+            pltpu.VMEM((n_slab, 8, BLOCK), f32),
         ]
         + [pltpu.VMEM(x.shape, x.dtype) for x in operands],
         compiler_params=pltpu.CompilerParams(

time: 54 us -> 53.6 us (level)
  no operation moved by 1% of the time
where the time goes in v2:
time: 53.6 us; the launch traced here: 53.4 us
  Pallas kernels  48 us (90%)
  local copies, waits for them, and re-layouts  4.7 us (9%)
  between operations  0.66 us (1%)
    pallas_call x1, Pallas kernels, body(): pl.pallas_call(functools.partial(kernel, n_slab, n_side), out_shape=(jax....  48 us
    unnamed x7, local copies, waits for them, and re-layouts  4.7 us

profile of v2, /device:TPU:0, one launch (start us, length us, event | category | flops | bytes accessed | tf_op | source)
XLA Modules:
  0.0 53.4 jit_solution(10319123503158307799)
XLA Ops:
  0.6 48.0 %shard_map.184 = (f32[19,4,64,128]{3,2,1,0:T(8,128)}, f32[3,1024]{1,0:T(4,128)}, f32[3,2048]{1,0:T(4,128)}) custom-call(f32[19,4,64,128]{3,2,1,0:T(8,128)} %pop_in.1, s32[4,64,128]{2,1,0:T(8,128)} %mask_in.1, s32[1,2048]{1,0:T(1,128)} %bitcast.8, s32[1,2048]{1,0:T(1,128)} %bitcast.9, s32[1,2048]{1,0:T(1,128)} %bitcast.10, f32[3,2048]{1,0:T(4,128)} %coords_in.1, ...), custom_call_target="tpu_custom_call" | custom-call | tf_op jit(solution)/shard_map/pallas_call | solution.py:645
  48.6 0.0 copy-start.1
  48.7 0.0 copy-start
  48.7 3.5 %copy.23 = f32[19,4,64,128]{3,2,1,0:T(8,128)} copy(f32[19,4,64,128]{3,2,1,0:T(8,128)} %get-tuple-element.6) | data formatting | bytes 4980736
  52.1 0.0 copy-done.1
  52.1 0.6 %copy.24 = f32[3,1024]{1,0:T(4,128)} copy(f32[3,1024]{1,0:T(4,128)S(1)} %copy-done.1) | data formatting | bytes 24576
  52.7 0.0 copy-done
  52.8 0.6 %copy.25 = f32[3,2048]{1,0:T(4,128)} copy(f32[3,2048]{1,0:T(4,128)S(1)} %copy-done) | data formatting | bytes 49152
Async XLA Ops:
  48.6 3.5 %copy-start.1 = (f32[3,1024]{1,0:T(4,128)S(1)}, f32[3,1024]{1,0:T(4,128)}, u32[]{:S(2)}) copy-start(f32[3,1024]{1,0:T(4,128)} %get-tuple-element.7) | copy-start | bytes 36868
  48.7 4.1 %copy-start = (f32[3,2048]{1,0:T(4,128)S(1)}, f32[3,2048]{1,0:T(4,128)}, u32[]{:S(2)}) copy-start(f32[3,2048]{1,0:T(4,128)} %get-tuple-element.8) | copy-start | bytes 73732

commit v3 on v2

--- a/solution.py
+++ b/solution.py
@@ -151,6 +151,8 @@
     psend,
     precv,
     hbuf,
+    moved,
+    out_sem,
     pop,
     mask,
     cell,
@@ -457,7 +459,7 @@
                 piece = padded[d, z + 1 - cz, PAD + x - cx : PAD + x - cx + 16, :]
                 if cy:
                     piece = pltpu.roll(piece, cy % span, 1)
-                out_pop[d, z, x : x + 16, :] = piece
+                moved[d, z, x : x + 16, :] = piece
                 density = piece if density is None else density + piece
                 for axis, c in enumerate((cx, cy, cz)):
                     if c:
@@ -472,6 +474,8 @@
         return carry
 
     lax.fori_loop(0, depth, stream, 0)
+    leaving = pltpu.make_async_copy(moved, out_pop, out_sem)
+    leaving.start()
 
     ready("cell", "normal")
     cells = depth * width
@@ -586,6 +590,7 @@
 
     for copy in halo_copies:
         copy.wait_send()
+    leaving.wait()
     departed(0, "slab", lambda peer: nbuf.at[side, slab])
     departed(1, "side", lambda peer: nbuf.at[side])
     departed(2, "side", lambda peer: lsend.at[peer])
@@ -650,7 +655,7 @@
             jax.ShapeDtypeStruct(iterate.shape, f32),
         ),
         in_specs=[pl.BlockSpec(memory_space=pltpu.HBM)] * len(operands),
-        out_specs=(vmem, vmem, vmem),
+        out_specs=(pl.BlockSpec(memory_space=pltpu.HBM), vmem, vmem),
         scratch_shapes=[
             pltpu.VMEM((directions, depth + 2, width + 2 * PAD, span), f32),
             pltpu.VMEM((4, depth * width, span), f32),
@@ -685,6 +690,8 @@
             pltpu.VMEM((n_slab, 3, SUB, BLOCK), f32),
             pltpu.VMEM((n_slab, 3, SUB, BLOCK), f32),
             pltpu.VMEM((n_slab, 8, BLOCK), f32),
+            pltpu.VMEM(populations.shape, f32),
+            DMA,
         ]
         + [pltpu.VMEM(x.shape, x.dtype) for x in operands],
         compiler_params=pltpu.CompilerParams(

time: 53.6 us -> 52.8 us (0.985)
  Pallas kernels: 48 us -> 47.2 us
    pallas_call x1, Pallas kernels: 48 us -> 47.2 us  [body(): pl.pallas_call(functools.partial(kernel, n_slab, n_side), out_shape=(jax....]
where the time goes in v3:
time: 52.8 us; the launch traced here: 52.5 us
  Pallas kernels  47.2 us (89%)
  local copies, waits for them, and re-layouts  4.7 us (9%)
  between operations  0.66 us (1%)
    pallas_call x1, Pallas kernels, body(): pl.pallas_call(functools.partial(kernel, n_slab, n_side), out_shape=(jax....  47.2 us
    unnamed x7, local copies, waits for them, and re-layouts  4.7 us

profile of v3, /device:TPU:0, one launch (start us, length us, event | category | flops | bytes accessed | tf_op | source)
XLA Modules:
  0.0 52.5 jit_solution(6081406547065647679)
XLA Ops:
  0.6 47.2 %shard_map.184 = (f32[19,4,64,128]{3,2,1,0:T(8,128)}, f32[3,1024]{1,0:T(4,128)}, f32[3,2048]{1,0:T(4,128)}) custom-call(f32[19,4,64,128]{3,2,1,0:T(8,128)} %pop_in.1, s32[4,64,128]{2,1,0:T(8,128)} %mask_in.1, s32[1,2048]{1,0:T(1,128)} %bitcast.8, s32[1,2048]{1,0:T(1,128)} %bitcast.9, s32[1,2048]{1,0:T(1,128)} %bitcast.10, f32[3,2048]{1,0:T(4,128)} %coords_in.1, ...), custom_call_target="tpu_custom_call" | custom-call | tf_op jit(solution)/shard_map/pallas_call | solution.py:650
  47.8 0.0 copy-start.1
  47.8 0.0 copy-start
  47.8 3.5 %copy.23 = f32[19,4,64,128]{3,2,1,0:T(8,128)} copy(f32[19,4,64,128]{3,2,1,0:T(8,128)} %get-tuple-element.6) | data formatting | bytes 4980736
  51.3 0.0 copy-done.1
  51.3 0.6 %copy.24 = f32[3,1024]{1,0:T(4,128)} copy(f32[3,1024]{1,0:T(4,128)S(1)} %copy-done.1) | data formatting | bytes 24576
  51.9 0.0 copy-done
  51.9 0.6 %copy.25 = f32[3,2048]{1,0:T(4,128)} copy(f32[3,2048]{1,0:T(4,128)S(1)} %copy-done) | data formatting | bytes 49152
Async XLA Ops:
  47.8 3.5 %copy-start.1 = (f32[3,1024]{1,0:T(4,128)S(1)}, f32[3,1024]{1,0:T(4,128)}, u32[]{:S(2)}) copy-start(f32[3,1024]{1,0:T(4,128)} %get-tuple-element.7) | copy-start | bytes 36868
  47.8 4.1 %copy-start = (f32[3,2048]{1,0:T(4,128)S(1)}, f32[3,2048]{1,0:T(4,128)}, u32[]{:S(2)}) copy-start(f32[3,2048]{1,0:T(4,128)} %get-tuple-element.8) | copy-start | bytes 73732
